TPU v7x, 32 devices: a whole 2x2x4 slice. The times are simulated.
32 devices in a mesh: chol: 4 (over y, x), pair: 8 (over z, core).
Axes of the slice: x: 2, y: 2, z: 4, core: 2. Of those that a mesh axis runs over, the one named last changes fastest.
Arguments:
- green: bfloat16 [2, 128, 147456], P(None, 'chol', 'pair'), may hold values from -6 to 6
- chol_rot: bfloat16 [147456, 1024], P('pair', 'chol'), may hold values from -0.015625 to 0.015625
Outputs:
- force_bias: float32 [2, 128, 1024], P(None, 'pair', 'chol')
All inputs are finite; a program needn't handle non-finite values.
Results may differ from a plain program's by a relative error of at most 0.0003.
Values may be sent and summed in bfloat16 or wider, within the bound.
A program may use at most 64 MiB of HBM per device.

v0:
```python
import jax
import jax.numpy as jnp
from jax import lax
from jax.sharding import PartitionSpec as P


def local(green, chol_rot):
    partial_value = jnp.einsum(
        "cwp,pg->wcg",
        lax.all_gather(green, "chol", axis=1, tiled=True),
        chol_rot,
        preferred_element_type=jnp.float32,
    )
    summed = lax.psum_scatter(partial_value, "pair", scatter_dimension=0, tiled=True)
    return jnp.transpose(summed, (1, 0, 2))


def solution(mesh):
    return jax.shard_map(
        local,
        mesh=mesh,
        in_specs=(P(None, "chol", "pair"), P("pair", "chol")),
        out_specs=P(None, "pair", "chol"),
        check_vma=False,
    )
```

profile of v0, /device:TPU:0, one launch (start us, length us, event | category | flops | bytes accessed | tf_op | source)
XLA Modules:
  0.0 182.8 jit_solution(14260340009630837000)
XLA Ops:
  6.5 0.0 all-gather.2.cloned.1.call-start
  6.5 0.7 all-gather.2.cloned.1.call-update
  7.3 0.0 copy-start
  7.3 0.0 all-reduce.3.cloned.1.call-start
  7.3 101.0 %all-gather.2.cloned.1.call-done = bf16[2,128,18432]{2,1,0:T(8,128)(2,1)} async-done(((bf16[2,32,18432]{2,1,0:T(8,128)(2,1)}), bf16[2,128,18432]{2,1,0:T(8,128)(2,1)}) %all-gather.2.cloned.1.call-update) | async-done | bytes 9437200 | tf_op jit(solution)/shard_map/all_gather | solution.py:10
  108.3 10.4 %fusion.2 = f32[128,2,256]{0,2,1:T(8,128)S(1)} fusion(bf16[2,128,18432]{2,1,0:T(8,128)(2,1)} %all-gather.2.cloned.1.call-done, bf16[18432,256]{1,0:T(8,128)(2,1)} %param.3), kind=kOutput, calls=%fused_computation.2 | convolution fusion | flops 2415919104 | bytes 19136512 | tf_op jit(solution)/shard_map/cwp,pg->wcg/dot_general | solution.py:8
  118.7 0.8 copy.6
  119.5 0.0 all-reduce.3.cloned.1.call-update
  119.5 0.0 copy-done
  119.6 0.6 dynamic-slice
  120.8 53.8 %all-reduce.3.cloned.1.call-done = f32[128,2,256]{2,1,0:T(2,128)} async-done(((f32[128,2,256]{2,1,0:T(2,128)}), f32[128,2,256]{2,1,0:T(2,128)}) %all-reduce.3.cloned.1.call-update) | async-done | bytes 262160
  174.6 0.8 dynamic-slice_bitcast_fusion
  175.3 0.6 copy.7
Async XLA Ops:
  6.5 101.7 %all-gather.2.cloned.1.call-start = ((), (), s32[]{:S(2)}) async-start(), calls=%async_computation | async-start | bytes 11796480 | tf_op jit(solution)/shard_map/all_gather | solution.py:10
  7.3 112.3 %copy-start = (u32[32]{0:T(128)S(1)}, u32[32]{0:T(128)}, u32[]{:S(2)}) copy-start(u32[32]{0:T(128)} %constant.2) | copy-start | bytes 388
  7.3 167.3 %all-reduce.3.cloned.1.call-start = ((), (), s32[]{:S(2)}) async-start(), calls=%async_computation.1 | async-start | bytes 524288
Sparse Core Ops, SparseCore 0:
  9.2 99.0 all-gather.1
  119.7 54.8 all-reduce.2
where the time goes:
time: 183 us
  waiting for transfers between devices  155 us (85%)
  between operations  14.1 us (8%)
  matrix products  10.4 us (6%)
  local copies, waits for them, and re-layouts  2.81 us (2%)
    all_gather x1, waiting for transfers between devices, local(): lax.all_gather(green, 'chol', axis=1, tiled=True)  101 us
    unnamed x3, waiting for transfers between devices  54.5 us
    dot_general x1, matrix products, local(): jnp.einsum('cwp,pg->wcg', lax.all_gather(green, 'chol', axis=1, tiled=Tru...  10.4 us
  transfers between devices with their start and end apart: 2, of which 2 were waited for; matrix products, arithmetic and copies ran while one was open for 0% of the time, Pallas kernels for 0%

commit v1 on v0

--- a/solution.py
+++ b/solution.py
@@ -4,12 +4,22 @@
 from jax.sharding import PartitionSpec as P
 
 
+def ring_gather(x, axis, dim):
+    ways = lax.axis_size(axis)
+    up = [(d, (d + 1) % ways) for d in range(ways)]
+    down = [(d, (d - 1) % ways) for d in range(ways)]
+    earlier, later = ([x], [x])
+    for _ in range(ways // 2):
+        earlier.append(lax.ppermute(earlier[-1], axis, up))
+    for _ in range((ways - 1) // 2):
+        later.append(lax.ppermute(later[-1], axis, down))
+    line = jnp.concatenate([*earlier[::-1], *later[1:]], axis=dim)
+    return jnp.roll(line, (lax.axis_index(axis) - ways // 2) * x.shape[dim], axis=dim)
+
+
 def local(green, chol_rot):
     partial_value = jnp.einsum(
-        "cwp,pg->wcg",
-        lax.all_gather(green, "chol", axis=1, tiled=True),
-        chol_rot,
-        preferred_element_type=jnp.float32,
+        "cwp,pg->wcg", ring_gather(green, "chol", 1), chol_rot, preferred_element_type=jnp.float32
     )
     summed = lax.psum_scatter(partial_value, "pair", scatter_dimension=0, tiled=True)
     return jnp.transpose(summed, (1, 0, 2))

time: 183 us -> 218 us (1.19)
  waiting for transfers between devices: 155 us -> 178 us
  local copies, waits for them, and re-layouts: 2.81 us -> 12.9 us
  starting transfers between devices: 0.04 us -> 5.87 us
  matrix products: 10.4 us -> 6.97 us
    ppermute x0 -> x3, waiting for transfers between devices: none -> 148 us  [the longest x2 105 us: ring_gather(): earlier.append(lax.ppermute(earlier[-1], axis, up))]
    all_gather x1 -> x0, waiting for transfers between devices: 101 us -> none  [local(): lax.all_gather(green, 'chol', axis=1, tiled=True)]
    unnamed x3 -> x1, waiting for transfers between devices: 54.5 us -> 0.02 us
    reduce_scatter x0 -> x1, waiting for transfers between devices: none -> 29.9 us  [local(): lax.psum_scatter(partial_value, 'pair', scatter_dimension=0, tiled=True)]
    unnamed x3 -> x9, local copies, waits for them, and re-layouts: 0.59 us -> 11.1 us
    ppermute x0 -> x3, starting transfers between devices: none -> 5.86 us  [the longest x2 3.66 us: ring_gather(): earlier.append(lax.ppermute(earlier[-1], axis, up))]
    dot_general x1, matrix products: 10.4 us -> 6.97 us  [local(): jnp.einsum('cwp,pg->wcg', ring_gather(green, 'chol', 1), chol_rot, prefer...]
    transpose x3 -> x0, local copies, waits for them, and re-layouts: 2.21 us -> none  [the longest x2 1.38 us: local(): return jnp.transpose(summed, (1, 0, 2))]
  transfers between devices with their start and end apart: 2 -> 4, of which waited for: 2 -> 4; matrix products, arithmetic and copies ran while one was open for 0% -> 3% of each run, Pallas kernels for 0% -> 0%
where the time goes in v1:
time: 218 us; the launch traced here: 217 us
  waiting for transfers between devices  178 us (82%)
  between operations  13.4 us (6%)
  local copies, waits for them, and re-layouts  12.9 us (6%)
  matrix products  6.97 us (3%)
  starting transfers between devices  5.87 us (3%)
    ppermute x2, waiting for transfers between devices, ring_gather(): earlier.append(lax.ppermute(earlier[-1], axis, up))  105 us
    ppermute x1, waiting for transfers between devices, ring_gather(): later.append(lax.ppermute(later[-1], axis, down))  43.2 us
    reduce_scatter x1, waiting for transfers between devices, local(): lax.psum_scatter(partial_value, 'pair', scatter_dimension=0, tiled=True)  29.9 us
    unnamed x9, local copies, waits for them, and re-layouts  11.1 us
    dot_general x1, matrix products, local(): jnp.einsum('cwp,pg->wcg', ring_gather(green, 'chol', 1), chol_rot, prefer...  6.97 us
  transfers between devices with their start and end apart: 4, of which 4 were waited for; matrix products, arithmetic and copies ran while one was open for 3% of the time, Pallas kernels for 0%

profile of v1, /device:TPU:0, one launch (start us, length us, event | category | flops | bytes accessed | tf_op | source)
XLA Modules:
  0.0 217.4 jit_solution(15633685500396896558)
XLA Ops:
  6.5 0.0 copy-start
  6.5 0.0 reduce-scatter.2.cloned.1.call-start
  6.5 2.9 %collective-permute-start = (bf16[2,32,18432]{2,1,0:T(8,128)(2,1)}, bf16[2,32,18432]{2,1,0:T(8,128)(2,1)}, u32[]{:S(2)}, u32[]{:S(2)}) collective-permute-start(bf16[2,32,18432]{2,1,0:T(8,128)(2,1)} %param.2), channel_id=1, source_target_pairs={{0,8},{8,16},{16,24},{24,0},{1,9},{9,17},{17,25},{25,1},{2,10},{10... | collective-permute-start | bytes 7077896 | tf_op jit(solution)/shard_map/ppermute | solution.py:13
  9.5 52.6 %collective-permute-done = bf16[2,32,18432]{2,1,0:T(8,128)(2,1)} collective-permute-done((bf16[2,32,18432]{2,1,0:T(8,128)(2,1)}, bf16[2,32,18432]{2,1,0:T(8,128)(2,1)}, u32[]{:S(2)}, u32[]{:S(2)}) %collective-permute-start) | collective-permute-done | bytes 2359328 | tf_op jit(solution)/shard_map/ppermute | solution.py:13
  62.1 0.7 collective-permute-start.1
  62.8 2.2 %collective-permute-start.2 = (bf16[2,32,18432]{2,1,0:T(8,128)(2,1)}, bf16[2,32,18432]{2,1,0:T(8,128)(2,1)}, u32[]{:S(2)}, u32[]{:S(2)}) collective-permute-start(bf16[2,32,18432]{2,1,0:T(8,128)(2,1)} %param.2), channel_id=1, source_target_pairs={{0,24},{8,0},{16,8},{24,16},{1,25},{9,1},{17,9},{25,17},{2,26},{10... | collective-permute-start | bytes 7077896 | tf_op jit(solution)/shard_map/ppermute | solution.py:15
  65.0 52.5 %collective-permute-done.1 = bf16[2,32,18432]{2,1,0:T(8,128)(2,1)} collective-permute-done((bf16[2,32,18432]{2,1,0:T(8,128)(2,1)}, bf16[2,32,18432]{2,1,0:T(8,128)(2,1)}, u32[]{:S(2)}, u32[]{:S(2)}) %collective-permute-start.1) | collective-permute-done | bytes 2359328 | tf_op jit(solution)/shard_map/ppermute | solution.py:13
  117.5 1.8 constant_dynamic-update-slice_fusion.7
  119.3 1.8 constant_dynamic-update-slice_fusion.6
  121.1 1.8 constant_dynamic-update-slice_fusion.5
  122.9 43.2 %collective-permute-done.2 = bf16[2,32,18432]{2,1,0:T(8,128)(2,1)} collective-permute-done((bf16[2,32,18432]{2,1,0:T(8,128)(2,1)}, bf16[2,32,18432]{2,1,0:T(8,128)(2,1)}, u32[]{:S(2)}, u32[]{:S(2)}) %collective-permute-start.2) | collective-permute-done | bytes 2359328 | tf_op jit(solution)/shard_map/ppermute | solution.py:15
  166.1 1.8 constant_dynamic-update-slice_fusion.4
  168.0 1.8 constant_dynamic-update-slice_fusion.3
  169.8 1.8 constant_dynamic-update-slice_fusion.2
  171.6 0.0 copy-done
  171.6 0.2 constant_dynamic-update-slice_fusion.1
  171.8 1.8 constant_dynamic-update-slice_fusion
  173.6 7.0 %fusion.3 = f32[128,2,256]{2,0,1:T(8,128)} fusion(bf16[18432,256]{1,0:T(8,128)(2,1)} %param.3, bf16[2,256,18432]{2,1,0:T(8,128)(2,1)S(1)} %constant_dynamic-update-slice_fusion, s32[]{:T(128)S(6)} %select_n.14), kind=kOutput, calls=%fused_computation.3 | convolution fusion | flops 2415919104 | bytes 19136516 | tf_op jit(solution)/shard_map/cwp,pg->wcg/dot_general | solution.py:21
  180.6 0.0 reduce-scatter.2.cloned.1.call-update
  180.6 29.9 %reduce-scatter.2.cloned.1.call-done = f32[16,2,256]{2,0,1:T(8,128)} async-done(((f32[128,2,256]{2,0,1:T(8,128)}), f32[16,2,256]{2,0,1:T(8,128)}) %reduce-scatter.2.cloned.1.call-update) | async-done | bytes 32784 | tf_op jit(solution)/shard_map/reduce_scatter | solution.py:24
Async XLA Ops:
  6.5 165.1 %copy-start = (bf16[2,32,18432]{2,1,0:T(8,128)(2,1)S(1)}, bf16[2,32,18432]{2,1,0:T(8,128)(2,1)}, u32[]{:S(2)}) copy-start(bf16[2,32,18432]{2,1,0:T(8,128)(2,1)} %param.2) | copy-start | bytes 7077892
  6.5 204.0 %reduce-scatter.2.cloned.1.call-start = ((), (), s32[]{:S(2)}) async-start(), calls=%async_computation.1 | async-start | bytes 294912 | tf_op jit(solution)/shard_map/reduce_scatter | solution.py:24
  6.5 55.5 %collective-permute-start = (bf16[2,32,18432]{2,1,0:T(8,128)(2,1)}, bf16[2,32,18432]{2,1,0:T(8,128)(2,1)}, u32[]{:S(2)}, u32[]{:S(2)}) collective-permute-start(bf16[2,32,18432]{2,1,0:T(8,128)(2,1)} %param.2), channel_id=1, source_target_pairs={{0,8},{8,16},{16,24},{24,0},{1,9},{9,17},{17,25},{25,1},{2,10},{10... | collective-permute-start | bytes 7077896 | tf_op jit(solution)/shard_map/ppermute | solution.py:13
  62.1 55.4 %collective-permute-start.1 = (bf16[2,32,18432]{2,1,0:T(8,128)(2,1)}, bf16[2,32,18432]{2,1,0:T(8,128)(2,1)}, u32[]{:S(2)}, u32[]{:S(2)}) collective-permute-start(bf16[2,32,18432]{2,1,0:T(8,128)(2,1)} %collective-permute-done), channel_id=1, source_target_pairs={{0,8},{8,16},{16,24},{24,0},{1,9},{9,17},{17,25},{25,1},{2,10},{10... | collective-permute-start | bytes 7077896 | tf_op jit(solution)/shard_map/ppermute | solution.py:13
  62.8 103.4 %collective-permute-start.2 = (bf16[2,32,18432]{2,1,0:T(8,128)(2,1)}, bf16[2,32,18432]{2,1,0:T(8,128)(2,1)}, u32[]{:S(2)}, u32[]{:S(2)}) collective-permute-start(bf16[2,32,18432]{2,1,0:T(8,128)(2,1)} %param.2), channel_id=1, source_target_pairs={{0,24},{8,0},{16,8},{24,16},{1,25},{9,1},{17,9},{25,17},{2,26},{10... | collective-permute-start | bytes 7077896 | tf_op jit(solution)/shard_map/ppermute | solution.py:15
Sparse Core Ops, SparseCore 0:
  180.7 29.7 reduce-scatter.1
